TPU v7x, 32 devices: a whole 2x2x4 slice. The times are simulated.
32 devices in a mesh: grp: 4 (over x, core), shard: 8 (over z, y).
Axes of the slice: x: 2, y: 2, z: 4, core: 2. Of those that a mesh axis runs over, the one named last changes fastest.
Arguments:
- query_states: bfloat16 [8192, 512], P(('grp', 'shard')), may hold values from -7.5 to 7.5
- key_states: bfloat16 [8192, 512], P(('grp', 'shard')), may hold values from -7.5 to 7.5
- value_states: bfloat16 [8192, 512], P(('grp', 'shard')), may hold values from -7.5 to 7.5
- valid_mask: int32 [8192], P(('grp', 'shard')), may hold values from 0 to 1, as said below
- attended_grad: bfloat16 [8192, 512], P(('grp', 'shard')), may hold values from -7.5 to 7.5
Outputs:
- attended: bfloat16 [8192, 512], P(('grp', 'shard'))
- query_grad: bfloat16 [8192, 512], P(('grp', 'shard'))
- key_grad: bfloat16 [8192, 512], P(('grp', 'shard'))
- value_grad: bfloat16 [8192, 512], P(('grp', 'shard'))
Inputs may be any that keep to these rules, and one draw needn't show every extreme that they name: `valid_mask`: in each device's run of 256 positions the ones form a prefix of 64 to 256 positions; the first run is all ones and the last has exactly 64.
All inputs are finite; a program needn't handle non-finite values.
Results may differ from a plain program's by a relative error of at most 0.0055.
Values may be sent and summed in bfloat16 or wider, within the bound.
A program may use at most 128 MiB of HBM per device.

v0:
```python
import functools

import jax
import jax.numpy as jnp
from jax import lax
from jax.experimental import pallas as pl
from jax.experimental.pallas import tpu as pltpu
from jax.sharding import PartitionSpec as P

HEADS = 4
HEAD_DIM = 128
BLOCK = 128
COARSE = 64
DIRECT = 5
TOK = 256
WIDTH = HEADS * HEAD_DIM
PACK = 2 * HEADS
TILE = PACK * COARSE
HALVES = 2
PART = PACK // HALVES
PART_HEADS = HEADS // HALVES
PART_TILE = PART * COARSE
PART_WIDTH = PART_HEADS * HEAD_DIM
SCALE = HEAD_DIM ** (-0.5)
MASKED = -1e30
DEAD = 1024.0
DEAD_SUM = 65536.0
MESH = pl.DeviceIdType.MESH
BF = jnp.bfloat16
F32 = jnp.float32


def rows_of(level):
    return COARSE >> level


def up_offset(level):
    return sum(PART * rows_of(i) for i in range(level))


def row_offset(level):
    return sum(rows_of(i) for i in range(level))


def iota(shape, dim):
    return lax.broadcasted_iota(jnp.int32, shape, dim)


def dot(a, b, dims):
    return lax.dot_general(a, b, (dims, ((), ())), preferred_element_type=F32)


NN = ((1,), (0,))
NT = ((1,), (1,))
TN = ((0,), (0,))


CHUNK = 64
NEAR = 4 * BLOCK


def level_row_maps(direct, shape, dim):
    idx = iota(shape, dim)
    low = jnp.full(shape, 2 * TOK, jnp.int32)
    size = jnp.ones(shape, jnp.int32)
    for level in range(direct):
        group = 4 << level
        at = row_offset(level)
        inside = (idx >= at) & (idx < at + rows_of(level))
        low = jnp.where(inside, (idx - at) * group, low)
        size = jnp.where(inside, group, size)
    return low, size


def kernel(
    n_grp, n_shard, direct, extra,
    q_in, k_in, v_in, m_in, c_in, *rest,
):
    if extra:
        xt_ref, *outs_hbm, xg_ref = rest[:6]
        rest = rest[6:]
    else:
        outs_hbm = rest[:4]
        rest = rest[4:]
    (att_ref, qg_ref, kg_ref, vg_ref, out_sem, q_ref, k_ref, v_ref, c_ref, m_ref, in_sem, kn, vn, up, far, ftile, small, mixed, mixed2, bias, score, dp,
     p_t, ds_t, own_g, edge_s, edge_r, gsend, grecv, gsum,
     halo_ss, halo_rs, up_ss, up_rs, ed_ss, ed_rs, dn_ss, dn_rs) = rest
    loads = [
        pltpu.make_async_copy(src, dst, in_sem.at[i])
        for i, (src, dst) in enumerate(
            ((k_in, k_ref), (v_in, v_ref), (q_in, q_ref), (c_in, c_ref), (m_in, m_ref)))
    ]
    for load in loads:
        load.start()
    stores = [
        pltpu.make_async_copy(src, dst, out_sem.at[i])
        for i, (src, dst) in enumerate(zip((att_ref, qg_ref, kg_ref, vg_ref), outs_hbm))
    ]
    n_dev = n_grp * n_shard
    me = lax.axis_index("grp") * n_shard + lax.axis_index("shard")
    span = 1 << direct
    far_rows = (direct + extra) * COARSE

    def where_is(dev):
        return (dev // n_shard, dev % n_shard)

    def sibling(level):
        part = me // (1 << level)
        return (part + 1 - 2 * (part % 2)) * (1 << level)

    base = (me // span) * span
    at_low = me == base
    at_high = me == base + span - 1
    has_prev = me > 0
    has_next = me < n_dev - 1
    out_prev = has_prev & at_low
    out_next = has_next & at_high
    barrier = pltpu.get_barrier_semaphore()

    def hello(t, _):
        pl.semaphore_signal(
            barrier, inc=1, device_id=where_is(base + (me - base + t) % span), device_id_type=MESH
        )
        return 0

    lax.fori_loop(1, span, hello, 0)
    if n_dev > span:
        @pl.when(out_prev)
        def _():
            pl.semaphore_signal(barrier, inc=1, device_id=where_is(me - 1), device_id_type=MESH)

        @pl.when(out_next)
        def _():
            pl.semaphore_signal(barrier, inc=1, device_id=where_is(me + 1), device_id_type=MESH)

    loads[0].wait()
    loads[1].wait()
    loads[4].wait()

    count = jnp.sum(m_ref[...], axis=1, keepdims=True)
    live_col = iota((TOK, 1), 0) < count
    kn[BLOCK:BLOCK + TOK, :] = jnp.where(live_col, k_ref[...].astype(F32), DEAD).astype(BF)
    vn[BLOCK:BLOCK + TOK, :] = v_ref[...]
    low, size = level_row_maps(direct, (128, TOK), 0)
    pos = iota((128, TOK), 1)
    pool = jnp.where((pos >= low) & (pos < low + size) & (pos < count), 1.0, 0.0).astype(BF)
    low_c, size_c = level_row_maps(direct, (128, 1), 0)
    row_count = jnp.clip(count - low_c, 0, size_c).astype(F32)
    row_div = jnp.maximum(row_count, 1.0)
    for half, part_pack in [(h, p) for h in range(HALVES) for p in range(PART)]:
        is_key = part_pack < PART_HEADS
        ref = k_ref if is_key else v_ref
        lane = (half * PART_HEADS + part_pack % PART_HEADS) * HEAD_DIM
        mean = dot(pool, ref[:, lane:lane + HEAD_DIM], NN) / row_div
        if is_key:
            mean = jnp.where(row_count > 0, mean, DEAD)
        for level in range(direct):
            rows = rows_of(level)
            part = mean[row_offset(level):row_offset(level) + rows]
            if rows >= 16:
                at = up_offset(level) + part_pack * rows
                up[half, at:at + rows, :] = part.astype(BF)
            else:
                at = up_offset(level) - up_offset(3) + part_pack * rows
                small[at:at + rows, :] = part
        if direct > 3 and part_pack == PART - 1:
            tail = up_offset(direct) - up_offset(3)
            up[half, up_offset(3):up_offset(direct), :] = small[0:tail, :].astype(BF)

    pl.semaphore_wait(barrier, span - 1)
    if n_dev > span:
        @pl.when(out_prev)
        def _():
            pl.semaphore_wait(barrier, 1)

        @pl.when(out_next)
        def _():
            pl.semaphore_wait(barrier, 1)

    def halo(half, which, side):
        ref = kn if which == 0 else vn
        slot = 4 * half + 2 * which + side
        wide = pl.ds(half * PART_WIDTH, PART_WIDTH)
        if side == 0:
            src, dst, dev = pl.ds(BLOCK, BLOCK), pl.ds(3 * BLOCK, BLOCK), me - 1
        else:
            src, dst, dev = pl.ds(2 * BLOCK, BLOCK), pl.ds(0, BLOCK), me + 1
        return pltpu.make_async_remote_copy(
            src_ref=ref.at[src, wide], dst_ref=ref.at[dst, wide],
            send_sem=halo_ss.at[slot], recv_sem=halo_rs.at[slot],
            device_id=where_is(dev), device_id_type=MESH,
        )

    def send_halo(half):
        @pl.when(has_prev)
        def _():
            halo(half, 0, 0).start()
            halo(half, 1, 0).start()

        @pl.when(has_next)
        def _():
            halo(half, 0, 1).start()
            halo(half, 1, 1).start()

    @pl.when(jnp.logical_not(has_prev))
    def _():
        kn[0:BLOCK, :] = jnp.full((BLOCK, WIDTH), DEAD, BF)
        vn[0:BLOCK, :] = jnp.zeros((BLOCK, WIDTH), BF)
        edge_r[0] = jnp.zeros((HALVES, BLOCK, WIDTH), BF)

    @pl.when(jnp.logical_not(has_next))
    def _():
        kn[3 * BLOCK:4 * BLOCK, :] = jnp.full((BLOCK, WIDTH), DEAD, BF)
        vn[3 * BLOCK:4 * BLOCK, :] = jnp.zeros((BLOCK, WIDTH), BF)
        edge_r[1] = jnp.zeros((HALVES, BLOCK, WIDTH), BF)

    def tile_at(half, level):
        return (half * direct + level) * PART_TILE

    def tile_ref(ref, half, level):
        return ref.at[tile_at(half, level):tile_at(half, level) + PART_TILE, :]

    def spread_out(half, level, source, target, send_sem, recv_sem):
        size = PART * rows_of(level)
        parts = 1 << level
        to = sibling(level)
        land = pl.multiple_of(tile_at(half, level) + (me % parts) * size, size)

        def send(t, _):
            m = (me + t) % parts
            pltpu.make_async_remote_copy(
                src_ref=source(m), dst_ref=target.at[pl.ds(land, size), :],
                send_sem=send_sem.at[half * direct + level],
                recv_sem=recv_sem.at[half * direct + level],
                device_id=where_is(to + m), device_id_type=MESH,
            ).start()
            return 0

        if parts == 1:
            send(0, 0)
        else:
            lax.fori_loop(0, parts, send, 0)

    for half in range(HALVES):
        send_halo(half)
        for level in reversed(range(direct)):
            at = up_offset(level)
            spread_out(
                half, level,
                lambda m, half=half, at=at, n=PART * rows_of(level): up.at[half, at:at + n, :],
                far, up_ss, up_rs,
            )

    loads[2].wait()
    loads[3].wait()
    block_col = iota((1, TOK), 1) // BLOCK

    def near_part(half):
        @pl.when(has_next)
        def _():
            halo(half, 0, 0).wait_recv()
            halo(half, 1, 0).wait_recv()

        @pl.when(has_prev)
        def _():
            halo(half, 0, 1).wait_recv()
            halo(half, 1, 1).wait_recv()

        for at in range(0, NEAR if half == 0 else 0, CHUNK):
            mark = jnp.where(
                kn[at:at + CHUNK, 0:HEAD_DIM].astype(F32)[:, 0:1] > DEAD / 2, MASKED, 0.0)
            mark = jnp.broadcast_to(mark, (CHUNK, TOK))
            if at < BLOCK:
                mark = jnp.where(block_col == 0, mark, MASKED)
            if at >= 3 * BLOCK:
                mark = jnp.where(block_col == 1, mark, MASKED)
            bias[at:at + CHUNK, :] = mark
        for head in range(half * PART_HEADS, (half + 1) * PART_HEADS):
            lane = slice(head * HEAD_DIM, (head + 1) * HEAD_DIM)
            score[head, 0:NEAR, :] = dot(kn[:, lane], q_ref[:, lane], NT)
            dp[head, 0:NEAR, :] = dot(vn[:, lane], c_ref[:, lane], NT)

    def pack_of(half, part_pack):
        head = half * PART_HEADS + part_pack % PART_HEADS
        return head if part_pack < PART_HEADS else HEADS + head

    def take_far(half):
        for level in range(direct):
            whole = tile_ref(far, half, level)
            pltpu.make_async_copy(whole, whole, up_rs.at[half * direct + level]).wait()
            rows = rows_of(level)
            at = level * COARSE
            if rows < 16:
                mixed[...] = whole[...].astype(F32)
            for part_pack in range(PART):
                pack = pack_of(half, part_pack)
                for m in range(1 << level):
                    src = (m * PART + part_pack) * rows
                    if rows >= 16:
                        src += tile_at(half, level)
                        ftile[pack, at + m * rows:at + (m + 1) * rows, :] = far[src:src + rows, :]
                    else:
                        small[m * rows:(m + 1) * rows, :] = mixed[src:src + rows, :]
                if rows < 16:
                    ftile[pack, at:at + COARSE, :] = small[0:COARSE, :].astype(BF)
        for e in range(extra):
            at = (direct + e) * COARSE
            for part_pack in range(PART):
                pack = pack_of(half, part_pack)
                ftile[pack, at:at + COARSE, :] = xt_ref[e, pack * COARSE:(pack + 1) * COARSE, :]
        for at in range(0, far_rows if half == 0 else 0, CHUNK):
            mark = jnp.where(
                ftile[0, at:at + CHUNK, :].astype(F32)[:, 0:1] > DEAD / 2, MASKED, 0.0)
            bias[NEAR + at:NEAR + at + CHUNK, :] = jnp.broadcast_to(mark, (CHUNK, TOK))

    def fold(value, op):
        return op(value.reshape(CHUNK // 8, 8, TOK), 0)

    def attend(head):
        lane = slice(head * HEAD_DIM, (head + 1) * HEAD_DIM)
        q = q_ref[:, lane]
        c = c_ref[:, lane]
        fk = ftile.at[head]
        fv = ftile.at[HEADS + head]
        score[head, NEAR:, :] = dot(fk[...], q, NT)
        dp[head, NEAR:, :] = dot(fv[...], c, NT)
        top = jnp.full((8, TOK), MASKED, F32)
        for at in range(0, NEAR + far_rows, CHUNK):
            t = score[head, at:at + CHUNK, :] * SCALE + bias[at:at + CHUNK, :]
            score[head, at:at + CHUNK, :] = t
            top = jnp.maximum(top, fold(t, jnp.max))
        top = jnp.max(top, 0, keepdims=True)
        z = jnp.zeros((8, TOK), F32)
        d = jnp.zeros((8, TOK), F32)
        for at in range(0, NEAR + far_rows, CHUNK):
            e = jnp.exp(score[head, at:at + CHUNK, :] - top)
            score[head, at:at + CHUNK, :] = e
            z = z + fold(e, jnp.sum)
            d = d + fold(e * dp[head, at:at + CHUNK, :], jnp.sum)
        inv = 1.0 / jnp.sum(z, 0, keepdims=True)
        delta = jnp.sum(d, 0, keepdims=True) * inv
        for at in range(0, NEAR + far_rows, CHUNK):
            p = score[head, at:at + CHUNK, :] * inv
            p_t[at:at + CHUNK, :] = p.astype(BF)
            ds_t[at:at + CHUNK, :] = (p * (dp[head, at:at + CHUNK, :] - delta)).astype(BF)
        gk = dot(ds_t[...], q, NN) * SCALE
        gv = dot(p_t[...], c, NN)
        half = head // PART_HEADS
        for part_pack, pack, g in (
            (head % PART_HEADS, head, gk), (PART_HEADS + head % PART_HEADS, HEADS + head, gv)
        ):
            wide = slice(pack * HEAD_DIM, (pack + 1) * HEAD_DIM)
            edge_wide = slice(part_pack * HEAD_DIM, (part_pack + 1) * HEAD_DIM)
            edge_s[0, half, :, edge_wide] = g[0:BLOCK].astype(BF)
            own_g[:, wide] = g[BLOCK:3 * BLOCK]
            edge_s[1, half, :, edge_wide] = g[3 * BLOCK:NEAR].astype(BF)
            for level in range(direct):
                at = NEAR + level * COARSE
                rows = rows_of(level)
                part = g[at:at + COARSE]
                if rows < 16:
                    small[0:COARSE, :] = part
                for m in range(1 << level):
                    dst = (m * PART + part_pack) * rows
                    if rows >= 16:
                        dst += tile_at(half, level)
                        gsend[dst:dst + rows, :] = part[m * rows:(m + 1) * rows].astype(BF)
                    else:
                        regrouped = mixed if level == 3 else mixed2
                        regrouped[dst:dst + rows, :] = small[m * rows:(m + 1) * rows, :]
            for e in range(extra):
                at = NEAR + (direct + e) * COARSE
                xg_ref[e, pack * COARSE:(pack + 1) * COARSE, :] = g[at:at + COARSE]
        out = dot(vn[:, lane], p_t[0:NEAR, :], TN) + dot(fv[...], p_t[NEAR:, :], TN)
        att_ref[:, lane] = out.T.astype(BF)
        out = dot(kn[:, lane], ds_t[0:NEAR, :], TN) + dot(fk[...], ds_t[NEAR:, :], TN)
        qg_ref[:, lane] = (out * SCALE).T.astype(BF)

    def edge(half, side):
        dev = me - 1 if side == 0 else me + 1
        return pltpu.make_async_remote_copy(
            src_ref=edge_s.at[side, half], dst_ref=edge_r.at[1 - side, half],
            send_sem=ed_ss.at[2 * half + side], recv_sem=ed_rs.at[2 * half + side],
            device_id=where_is(dev), device_id_type=MESH,
        )

    def send_back(half):
        @pl.when(has_prev)
        def _():
            edge(half, 0).start()

        @pl.when(has_next)
        def _():
            edge(half, 1).start()

        for level in reversed(range(direct)):
            at = tile_at(half, level)
            if rows_of(level) < 16:
                regrouped = mixed if level == 3 else mixed2
                gsend[at:at + PART_TILE, :] = regrouped[...].astype(BF)
            size = PART * rows_of(level)
            spread_out(
                half, level,
                lambda m, at=at, n=size: gsend.at[pl.ds(pl.multiple_of(at + m * n, n), n), :],
                grecv, dn_ss, dn_rs,
            )

    near_part(0)
    for half in range(HALVES):
        take_far(half)
        for head in range(half * PART_HEADS, (half + 1) * PART_HEADS):
            attend(head)
        send_back(half)
        if half + 1 < HALVES:
            near_part(half + 1)

    stores[0].start()
    stores[1].start()
    low_p, size_p = level_row_maps(direct, (TOK, 128), 1)
    pos_p = iota((TOK, 128), 0)
    share = jnp.where(
        (pos_p >= low_p) & (pos_p < low_p + size_p) & (pos_p < count), 1.0, 0.0
    ).astype(BF)
    share = jnp.concatenate([share, share], axis=1)

    gsum[:, row_offset(direct):, :] = jnp.zeros((PACK, 128 - row_offset(direct), 128), F32)
    for half in range(HALVES):
        for level in range(direct):
            whole = tile_ref(grecv, half, level)
            pltpu.make_async_copy(whole, whole, dn_rs.at[half * direct + level]).wait()
            rows = rows_of(level)
            n = PART * rows
            at = tile_at(half, level)
            total = grecv[at:at + n, :].astype(F32)
            for m in range(1, 1 << level):
                total = total + grecv[at + m * n:at + (m + 1) * n, :].astype(F32)
            at = row_offset(level)
            if rows < 8:
                small[0:n, :] = total
            for part_pack in range(PART):
                cut = slice(part_pack * rows, (part_pack + 1) * rows)
                pack = pack_of(half, part_pack)
                gsum[pack, at:at + rows, :] = total[cut] if rows >= 8 else small[cut, :]

        @pl.when(has_next)
        def _():
            edge(half, 0).wait_recv()

        @pl.when(has_prev)
        def _():
            edge(half, 1).wait_recv()

        for part_pack in range(PART):
            pack = pack_of(half, part_pack)
            wide = slice(pack * HEAD_DIM, (pack + 1) * HEAD_DIM)
            lane = slice((pack % HEADS) * HEAD_DIM, (pack % HEADS + 1) * HEAD_DIM)
            cut = slice(part_pack * HEAD_DIM, (part_pack + 1) * HEAD_DIM)
            g = gsum[pack] / row_div
            high = g.astype(BF)
            rest_g = (g - high.astype(F32)).astype(BF)
            total = own_g[:, wide] + dot(share, jnp.concatenate([high, rest_g], axis=0), NN)
            total = total + jnp.concatenate(
                [edge_r[0, half, :, cut], edge_r[1, half, :, cut]], 0).astype(F32)
            out = kg_ref if pack < HEADS else vg_ref
            out[:, lane] = total.astype(out.dtype)
    stores[2].start()
    stores[3].start()

    for half in range(HALVES):
        @pl.when(has_prev)
        def _():
            halo(half, 0, 0).wait_send()
            halo(half, 1, 0).wait_send()
            edge(half, 0).wait_send()

        @pl.when(has_next)
        def _():
            halo(half, 0, 1).wait_send()
            halo(half, 1, 1).wait_send()
            edge(half, 1).wait_send()

        for level in range(direct):
            whole = tile_ref(far, half, level)
            pltpu.make_async_copy(whole, whole, up_ss.at[half * direct + level]).wait()
            whole = tile_ref(grecv, half, level)
            pltpu.make_async_copy(whole, whole, dn_ss.at[half * direct + level]).wait()
    for store in stores:
        store.wait()


def deliver(*refs):
    held, in_sem, out_sem = refs[8:]
    ins = [pltpu.make_async_copy(refs[i], held.at[i], in_sem.at[i]) for i in range(4)]
    outs = [pltpu.make_async_copy(held.at[i], refs[4 + i], out_sem.at[i]) for i in range(4)]
    for copy in ins:
        copy.start()
    for i in range(4):
        ins[i].wait()
        outs[i].start()
    for copy in outs:
        copy.wait()


def swapped(block, axis, stride):
    count = lax.axis_size(axis)
    route = [(i, i ^ (1 << stride)) for i in range(count)]
    return lax.ppermute(block, axis, route)


def halved(lower, upper):
    both = jnp.concatenate([lower, upper], axis=0)
    return both.reshape((both.shape[0] // 2, 2) + both.shape[1:]).sum(axis=1)


def ordered(side, own, other):
    return jnp.where(side == 0, own, other), jnp.where(side == 0, other, own)


def level_axes():
    shard_bits = lax.axis_size("shard").bit_length() - 1
    grp_bits = lax.axis_size("grp").bit_length() - 1
    return [("shard", i) for i in range(shard_bits)] + [("grp", i) for i in range(grp_bits)]


def climb(key_states, value_states, valid_mask, axes, direct):
    mask = valid_mask.astype(F32)
    kv = jnp.concatenate([key_states, value_states], axis=1).astype(F32)
    tile = (kv * mask[:, None]).reshape(COARSE, -1, 2 * WIDTH).sum(axis=1)
    count = mask.reshape(COARSE, -1).sum(axis=1)
    tiles = []
    counts = []
    for level, (axis, bit) in enumerate(axes):
        side = lax.axis_index(axis) >> bit & 1
        other, other_count = swapped((tile, count), axis, bit)
        if level >= direct:
            mean = (other / jnp.maximum(other_count, 1.0)[:, None]).astype(BF)
            marked = jnp.where(other_count[:, None] > 0, mean[:, :WIDTH], jnp.asarray(DEAD, BF))
            mean = jnp.concatenate([marked, mean[:, WIDTH:]], axis=1)
            tiles.append(
                mean.reshape(COARSE, PACK, HEAD_DIM).transpose(1, 0, 2).reshape(TILE, HEAD_DIM))
            counts.append(other_count)
        tile = halved(*ordered(side, tile, other))
        count = halved(*ordered(side, count, other_count))
    return jnp.stack(tiles), jnp.stack(counts)


def descend(grads, counts, axes, direct):
    zero = jnp.zeros((COARSE, 2 * WIDTH), F32)
    own = zero
    for level in reversed(range(len(axes))):
        axis, bit = axes[level]
        side = lax.axis_index(axis) >> bit & 1
        wide = jnp.repeat(own, 2, axis=0)
        mine, theirs = ordered(side, wide[:COARSE], wide[COARSE:])
        if level >= direct:
            part = grads[level - direct].reshape(PACK, COARSE, HEAD_DIM).transpose(1, 0, 2)
            part = part.reshape(COARSE, 2 * WIDTH)
            theirs = theirs + part / jnp.maximum(counts[level - direct], 1.0)[:, None]
        own = mine + swapped(theirs, axis, bit)
    return own


def body(query_states, key_states, value_states, valid_mask, attended_grad):
    axes = level_axes()
    n_grp = lax.axis_size("grp")
    n_shard = lax.axis_size("shard")
    direct = min(DIRECT, len(axes))
    extra = len(axes) - direct
    operands = [
        query_states, key_states, value_states, valid_mask.reshape(1, TOK), attended_grad]
    grad_type = F32 if extra else BF
    outs = [jax.ShapeDtypeStruct((TOK, WIDTH), t) for t in (BF, BF, grad_type, grad_type)]
    if extra:
        tiles, counts = climb(key_states, value_states, valid_mask, axes, direct)
        operands.append(tiles)
        outs.append(jax.ShapeDtypeStruct((extra, TILE, HEAD_DIM), F32))
    vmem = pl.BlockSpec(memory_space=pltpu.VMEM)
    hbm = pl.BlockSpec(memory_space=pltpu.HBM)
    dma = pltpu.SemaphoreType.DMA
    all_rows = NEAR + (direct + extra) * COARSE
    results = pl.pallas_call(
        functools.partial(kernel, n_grp, n_shard, direct, extra),
        out_shape=outs,
        in_specs=[hbm] * 5 + [vmem] * (len(operands) - 5),
        out_specs=[hbm] * 4 + [vmem] * (len(outs) - 4),
        scratch_shapes=[
            pltpu.VMEM((TOK, WIDTH), BF),
            pltpu.VMEM((TOK, WIDTH), BF),
            pltpu.VMEM((TOK, WIDTH), grad_type),
            pltpu.VMEM((TOK, WIDTH), grad_type),
            dma((4,)),
            pltpu.VMEM((TOK, WIDTH), BF),
            pltpu.VMEM((TOK, WIDTH), BF),
            pltpu.VMEM((TOK, WIDTH), BF),
            pltpu.VMEM((TOK, WIDTH), BF),
            pltpu.VMEM((1, TOK), jnp.int32),
            dma((5,)),
            pltpu.VMEM((NEAR, WIDTH), BF),
            pltpu.VMEM((NEAR, WIDTH), BF),
            pltpu.VMEM((HALVES, up_offset(direct), HEAD_DIM), BF),
            pltpu.VMEM((direct * TILE, HEAD_DIM), BF),
            pltpu.VMEM((PACK, (direct + extra) * COARSE, HEAD_DIM), BF),
            pltpu.VMEM((128, HEAD_DIM), F32),
            pltpu.VMEM((PART_TILE, HEAD_DIM), F32),
            pltpu.VMEM((PART_TILE, HEAD_DIM), F32),
            pltpu.VMEM((all_rows, TOK), F32),
            pltpu.VMEM((HEADS, all_rows, TOK), F32),
            pltpu.VMEM((HEADS, all_rows, TOK), F32),
            pltpu.VMEM((all_rows, TOK), BF),
            pltpu.VMEM((all_rows, TOK), BF),
            pltpu.VMEM((TOK, 2 * WIDTH), F32),
            pltpu.VMEM((2, HALVES, BLOCK, WIDTH), BF),
            pltpu.VMEM((2, HALVES, BLOCK, WIDTH), BF),
            pltpu.VMEM((direct * TILE, HEAD_DIM), BF),
            pltpu.VMEM((direct * TILE, HEAD_DIM), BF),
            pltpu.VMEM((PACK, 128, HEAD_DIM), F32),
            dma((4 * HALVES,)),
            dma((4 * HALVES,)),
            dma((HALVES * direct,)),
            dma((HALVES * direct,)),
            dma((2 * HALVES,)),
            dma((2 * HALVES,)),
            dma((HALVES * direct,)),
            dma((HALVES * direct,)),
        ],
        compiler_params=pltpu.CompilerParams(
            collective_id=0, has_side_effects=True, vmem_limit_bytes=63 * 1024 * 1024
        ),
    )(*operands)
    if not extra:
        return pl.pallas_call(
            deliver,
            out_shape=outs,
            in_specs=[hbm] * 4,
            out_specs=[hbm] * 4,
            scratch_shapes=[pltpu.VMEM((4, TOK, WIDTH), BF), dma((4,)), dma((4,))],
            compiler_params=pltpu.CompilerParams(vmem_limit_bytes=63 * 1024 * 1024),
        )(*results)
    attended, query_grad, key_grad, value_grad, grads = results
    own = descend(grads, counts, axes, direct)
    spread = jnp.repeat(own, TOK // COARSE, axis=0) * valid_mask.astype(F32)[:, None]
    return (
        attended,
        query_grad,
        (key_grad + spread[:, :WIDTH]).astype(BF),
        (value_grad + spread[:, WIDTH:]).astype(BF),
    )


def solution(mesh):
    rows = P(("grp", "shard"), None)
    return jax.shard_map(
        body,
        mesh=mesh,
        in_specs=(rows, rows, rows, P(("grp", "shard")), rows),
        out_specs=(rows, rows, rows, rows),
        check_vma=False,
    )
```

profile of v0, /device:TPU:0, one launch (start us, length us, event | category | flops | bytes accessed | tf_op | source)
XLA Modules:
  0.0 50.5 jit_solution(12522388826927563722)
XLA Ops:
  0.6 47.9 %shard_map.84 = (bf16[256,512]{1,0:T(8,128)(2,1)}, bf16[256,512]{1,0:T(8,128)(2,1)}, bf16[256,512]{1,0:T(8,128)(2,1)}, bf16[256,512]{1,0:T(8,128)(2,1)}) custom-call(bf16[256,512]{1,0:T(8,128)(2,1)} %q_in.1, bf16[256,512]{1,0:T(8,128)(2,1)} %k_in.1, bf16[256,512]{1,0:T(8,128)(2,1)} %v_in.1, s32[1,256]{1,0:T(1,128)} %bitcast.1, bf16[256,512]{1,0:T(8,128)(2,1)} %c_in.1), custom_call_target="tpu_custom_call" | custom-call | tf_op jit(solution)/shard_map/pallas_call | solution.py:581
  48.5 2.0 %shard_map.85 = (bf16[256,512]{1,0:T(8,128)(2,1)}, bf16[256,512]{1,0:T(8,128)(2,1)}, bf16[256,512]{1,0:T(8,128)(2,1)}, bf16[256,512]{1,0:T(8,128)(2,1)}) custom-call(bf16[256,512]{1,0:T(8,128)(2,1)} %get-tuple-element.8.refs_0_, bf16[256,512]{1,0:T(8,128)(2,1)} %get-tuple-element.9.refs_1_, bf16[256,512]{1,0:T(8,128)(2,1)} %get-tuple-element.10.refs_2_, ...), custom_call_target="tpu_custom_call" | custom-call | tf_op jit(solution)/shard_map/pallas_call | solution.py:631
where the time goes:
time: 51.4 us; the launch traced here: 50.5 us
  Pallas kernels  49.9 us (97%)
  between operations  0.64 us (1%)
    pallas_call x1, Pallas kernels, body(): pl.pallas_call(functools.partial(kernel, n_grp, n_shard, direct, extra),...  47.9 us
    pallas_call x1, Pallas kernels, body(): pl.pallas_call(deliver, out_shape=outs, in_specs=[hbm] * 4, out_specs=[hb...  1.98 us

commit v1 on v0

--- a/solution.py
+++ b/solution.py
@@ -84,7 +84,7 @@
         rest = rest[4:]
     (att_ref, qg_ref, kg_ref, vg_ref, out_sem, q_ref, k_ref, v_ref, c_ref, m_ref, in_sem, kn, vn, up, far, ftile, small, mixed, mixed2, bias, score, dp,
      p_t, ds_t, own_g, edge_s, edge_r, gsend, grecv, gsum,
-     halo_ss, halo_rs, up_ss, up_rs, ed_ss, ed_rs, dn_ss, dn_rs) = rest
+     halo_ss, halo_rs, hop_ss, hop_rs, up_ss, up_rs, ed_ss, ed_rs, dn_ss, dn_rs) = rest
     loads = [
         pltpu.make_async_copy(src, dst, in_sem.at[i])
         for i, (src, dst) in enumerate(
@@ -241,9 +241,55 @@
         else:
             lax.fori_loop(0, parts, send, 0)
 
+    def first_hop(half, level):
+        size = PART * rows_of(level)
+        parts = 1 << level
+        fours = parts // 4
+        at = up_offset(level)
+        to = sibling(level)
+        land = pl.multiple_of(tile_at(half, level) + (me % parts) * size, size)
+
+        def send(t, _):
+            m = me % 4 + 4 * ((me // 4 + t) % fours)
+            pltpu.make_async_remote_copy(
+                src_ref=up.at[half, at:at + size, :], dst_ref=far.at[pl.ds(land, size), :],
+                send_sem=hop_ss.at[half * direct + level],
+                recv_sem=hop_rs.at[half * direct + level],
+                device_id=where_is(to + m), device_id_type=MESH,
+            ).start()
+            return 0
+
+        lax.fori_loop(0, fours, send, 0)
+
+    def second_hop(half):
+        for level in reversed(range(2, direct)):
+            size = PART * rows_of(level)
+            at = tile_at(half, level)
+            whole = far.at[at:at + PART_TILE // 4, :]
+            pltpu.make_async_copy(whole, whole, hop_rs.at[half * direct + level]).wait()
+
+            def send(t, _):
+                land = pl.multiple_of(at + (me % 4 + 4 * (t // 3)) * size, size)
+                pltpu.make_async_remote_copy(
+                    src_ref=far.at[pl.ds(land, size), :], dst_ref=far.at[pl.ds(land, size), :],
+                    send_sem=up_ss.at[half * direct + level],
+                    recv_sem=up_rs.at[half * direct + level],
+                    device_id=where_is((me // 4) * 4 + (me + 1 + t % 3) % 4),
+                    device_id_type=MESH,
+                ).start()
+                return 0
+
+            lax.fori_loop(0, 3 * ((1 << level) // 4), send, 0)
+
+    def up_ref(half, level):
+        at = tile_at(half, level)
+        return far.at[at:at + (PART_TILE if level < 2 else 3 * (PART_TILE // 4)), :]
+
     for half in range(HALVES):
+        for level in reversed(range(2, direct)):
+            first_hop(half, level)
         send_halo(half)
-        for level in reversed(range(direct)):
+        for level in reversed(range(min(2, direct))):
             at = up_offset(level)
             spread_out(
                 half, level,
@@ -286,8 +332,9 @@
 
     def take_far(half):
         for level in range(direct):
+            landed = up_ref(half, level)
+            pltpu.make_async_copy(landed, landed, up_rs.at[half * direct + level]).wait()
             whole = tile_ref(far, half, level)
-            pltpu.make_async_copy(whole, whole, up_rs.at[half * direct + level]).wait()
             rows = rows_of(level)
             at = level * COARSE
             if rows < 16:
@@ -405,7 +452,9 @@
                 grecv, dn_ss, dn_rs,
             )
 
+    second_hop(0)
     near_part(0)
+    second_hop(1)
     for half in range(HALVES):
         take_far(half)
         for head in range(half * PART_HEADS, (half + 1) * PART_HEADS):
@@ -480,8 +529,11 @@
             edge(half, 1).wait_send()
 
         for level in range(direct):
-            whole = tile_ref(far, half, level)
+            whole = up_ref(half, level)
             pltpu.make_async_copy(whole, whole, up_ss.at[half * direct + level]).wait()
+            if level >= 2:
+                whole = far.at[0:PART_TILE // 4, :]
+                pltpu.make_async_copy(whole, whole, hop_ss.at[half * direct + level]).wait()
             whole = tile_ref(grecv, half, level)
             pltpu.make_async_copy(whole, whole, dn_ss.at[half * direct + level]).wait()
     for store in stores:
@@ -618,6 +670,8 @@
             dma((4 * HALVES,)),
             dma((HALVES * direct,)),
             dma((HALVES * direct,)),
+            dma((HALVES * direct,)),
+            dma((HALVES * direct,)),
             dma((2 * HALVES,)),
             dma((2 * HALVES,)),
             dma((HALVES * direct,)),

time: 51.4 us -> 53.5 us (1.041); the launches traced: 50.5 us -> 53.4 us
  Pallas kernels: 49.9 us -> 52.7 us
    pallas_call x1, Pallas kernels: 47.9 us -> 50.7 us  [body(): pl.pallas_call(functools.partial(kernel, n_grp, n_shard, direct, extra),...]
where the time goes in v1:
time: 53.5 us; the launch traced here: 53.4 us
  Pallas kernels  52.7 us (99%)
  between operations  0.64 us (1%)
    pallas_call x1, Pallas kernels, body(): pl.pallas_call(functools.partial(kernel, n_grp, n_shard, direct, extra),...  50.7 us
    pallas_call x1, Pallas kernels, body(): pl.pallas_call(deliver, out_shape=outs, in_specs=[hbm] * 4, out_specs=[hb...  1.98 us

profile of v1, /device:TPU:0, one launch (start us, length us, event | category | flops | bytes accessed | tf_op | source)
XLA Modules:
  0.0 53.4 jit_solution(13110049836317867611)
XLA Ops:
  0.6 50.7 %shard_map.84 = (bf16[256,512]{1,0:T(8,128)(2,1)}, bf16[256,512]{1,0:T(8,128)(2,1)}, bf16[256,512]{1,0:T(8,128)(2,1)}, bf16[256,512]{1,0:T(8,128)(2,1)}) custom-call(bf16[256,512]{1,0:T(8,128)(2,1)} %q_in.1, bf16[256,512]{1,0:T(8,128)(2,1)} %k_in.1, bf16[256,512]{1,0:T(8,128)(2,1)} %v_in.1, s32[1,256]{1,0:T(1,128)} %bitcast.1, bf16[256,512]{1,0:T(8,128)(2,1)} %c_in.1), custom_call_target="tpu_custom_call" | custom-call | tf_op jit(solution)/shard_map/pallas_call | solution.py:633
  51.4 2.0 %shard_map.85 = (bf16[256,512]{1,0:T(8,128)(2,1)}, bf16[256,512]{1,0:T(8,128)(2,1)}, bf16[256,512]{1,0:T(8,128)(2,1)}, bf16[256,512]{1,0:T(8,128)(2,1)}) custom-call(bf16[256,512]{1,0:T(8,128)(2,1)} %get-tuple-element.8.refs_0_, bf16[256,512]{1,0:T(8,128)(2,1)} %get-tuple-element.9.refs_1_, bf16[256,512]{1,0:T(8,128)(2,1)} %get-tuple-element.10.refs_2_, ...), custom_call_target="tpu_custom_call" | custom-call | tf_op jit(solution)/shard_map/pallas_call | solution.py:685
